TPU v7x, 32 devices: a whole 2x2x4 slice. The times are simulated.
32 devices in a mesh: dp: 4 (over x, core), term: 8 (over z, y).
Axes of the slice: x: 2, y: 2, z: 4, core: 2. Of those that a mesh axis runs over, the one named last changes fastest.
Arguments:
- inputs: bfloat16 [1024, 8192], P('dp'), may hold values from -6 to 6
- cotangent: bfloat16 [1024, 8192], P('dp', 'term'), may hold values from -6 to 6
- logits: float32 [1024, 256], P('dp'), may hold values from -20 to 320
- in_factor: bfloat16 [8192, 2048], P(None, 'term'), may hold values from -0.09375 to 0.09375
- out_factor: bfloat16 [8192, 2048], P(None, 'term'), may hold values from -0.0625 to 0.0625
- expert_factor: bfloat16 [256, 2048], P(None, 'term'), may hold values from -3 to 3
Outputs:
- grad_inputs: bfloat16 [1024, 8192], P('dp', 'term')
- grad_logits: float32 [1024, 256], P('dp', 'term')
- grad_in_factor: float32 [8192, 2048], P('dp', 'term')
- grad_out_factor: float32 [8192, 2048], P('dp', 'term')
- grad_expert_factor: float32 [256, 2048], P('dp', 'term')
All inputs are finite; a program needn't handle non-finite values.
Results may differ from a plain program's by a relative error of at most 0.028.
Values may be sent and summed in bfloat16 or wider, within the bound.
A program may use at most 128 MiB of HBM per device.

v0:
```python
import math

import jax
import jax.numpy as jnp
from jax import lax
from jax.sharding import PartitionSpec as P


def per_device(inputs, cotangent, logits, in_factor, out_factor, expert_factor):
    fl = jnp.float32
    n_term = lax.axis_size("term")
    n_data = lax.axis_size("dp")
    gates = jax.nn.softmax(logits, axis=-1)
    gates_bf = gates.astype(jnp.bfloat16)
    proj_in = jnp.dot(inputs, in_factor, preferred_element_type=fl)
    proj_exp = jnp.dot(gates_bf, expert_factor, preferred_element_type=fl)
    hidden = (proj_in * proj_exp).astype(jnp.bfloat16)
    full_cotan = lax.all_gather(cotangent, "term", axis=1, tiled=True)
    grad_hid = jnp.dot(full_cotan, out_factor, preferred_element_type=fl)
    grad_pin = (grad_hid * proj_exp).astype(jnp.bfloat16)
    grad_pexp = (grad_hid * proj_in).astype(jnp.bfloat16)
    row_total = lax.psum(jnp.sum(grad_hid * proj_in * proj_exp, axis=1, keepdims=True), "term")
    contract_last = (((1,), (1,)), ((), ()))
    part_x = lax.dot_general(grad_pin, in_factor, contract_last, preferred_element_type=fl)
    part_g = lax.dot_general(grad_pexp, expert_factor, contract_last, preferred_element_type=fl)
    sum_x, grad_gate = (
        lax.psum_scatter(
            part_x.astype(jnp.bfloat16), "term", scatter_dimension=1, tiled=True
        ).astype(jnp.float32),
        lax.psum_scatter(
            part_g.astype(jnp.bfloat16), "term", scatter_dimension=1, tiled=True
        ).astype(jnp.float32),
    )
    grad_inputs = sum_x.astype(jnp.bfloat16)
    exp_local = logits.shape[1] // n_term
    gates_local = lax.dynamic_slice_in_dim(gates, lax.axis_index("term") * exp_local, exp_local, 1)
    grad_logits = gates_local * (grad_gate - row_total)
    scale = 1.0 / math.sqrt(inputs.shape[0] * n_data)
    contract_first = (((0,), (0,)), ((), ()))
    part_in = lax.dot_general(inputs, grad_pin, contract_first, preferred_element_type=fl) * scale
    part_out = (
        lax.dot_general(full_cotan, hidden, contract_first, preferred_element_type=fl) * scale
    )
    part_exp = (
        lax.dot_general(gates_bf, grad_pexp, contract_first, preferred_element_type=fl) * scale
    )
    grad_in, grad_out, grad_exp = (
        lax.psum_scatter(
            part_in.astype(jnp.bfloat16), "dp", scatter_dimension=0, tiled=True
        ).astype(jnp.float32),
        lax.psum_scatter(
            part_out.astype(jnp.bfloat16), "dp", scatter_dimension=0, tiled=True
        ).astype(jnp.float32),
        lax.psum_scatter(
            part_exp.astype(jnp.bfloat16), "dp", scatter_dimension=0, tiled=True
        ).astype(jnp.float32),
    )
    return (grad_inputs, grad_logits, grad_in, grad_out, grad_exp)


def solution(mesh):
    return jax.shard_map(
        per_device,
        mesh=mesh,
        in_specs=(
            P("dp", None),
            P("dp", "term"),
            P("dp", None),
            P(None, "term"),
            P(None, "term"),
            P(None, "term"),
        ),
        out_specs=(
            P("dp", "term"),
            P("dp", "term"),
            P("dp", "term"),
            P("dp", "term"),
            P("dp", "term"),
        ),
        check_vma=False,
    )
```

profile of v0, /device:TPU:0, one launch (start us, length us, event | category | flops | bytes accessed | tf_op | source)
XLA Modules:
  0.0 368.6 jit_solution(12951424411813804137)
XLA Ops:
  7.2 0.7 all-gather.2.cloned.1.call-update
  8.0 1.1 copy.11
  9.1 1.1 reduce_max.9
  10.1 0.1 fusion.6
  10.2 5.2 %fusion.11 = f32[256,256]{0,1:T(8,128)S(1)} fusion(bf16[256,8192]{1,0:T(8,128)(2,1)} %param.6, bf16[8192,256]{1,0:T(8,128)(2,1)} %param.9), kind=kOutput, calls=%fused_computation.22 | convolution fusion | flops 1073741824 | bytes 8650752 | tf_op jit(solution)/shard_map/dot_general | solution.py:15
  15.5 70.9 %all-gather.2.cloned.1.call-done = bf16[256,8192]{1,0:T(8,128)(2,1)} async-done(((bf16[256,1024]{1,0:T(8,128)(2,1)}), bf16[256,8192]{1,0:T(8,128)(2,1)}) %all-gather.2.cloned.1.call-update) | async-done | bytes 4194320 | tf_op jit(solution)/shard_map/all_gather | solution.py:18
  86.3 5.2 %fusion.10 = f32[256,256]{0,1:T(8,128)S(1)} fusion(bf16[256,8192]{1,0:T(8,128)(2,1)} %all-gather.2.cloned.1.call-done, bf16[8192,256]{1,0:T(8,128)(2,1)} %param.10), kind=kOutput, calls=%fused_computation.21 | convolution fusion | flops 1073741824 | bytes 8650752 | tf_op jit(solution)/shard_map/dot_general | solution.py:19
  91.5 0.3 multiply_reduce_fusion
  91.8 0.9 fusion.4
  92.7 0.0 reduce-scatter.8.cloned.1.call-start
  92.7 0.8 convolution_convert_fusion.1
  93.7 5.4 %fusion.2 = bf16[8192,256]{0,1:T(8,128)(2,1)} fusion(bf16[256,8192]{1,0:T(8,128)(2,1)} %all-gather.2.cloned.1.call-done, f32[256,256]{0,1:T(8,128)S(1)} %fusion.11, f32[256,256]{0,1:T(8,128)S(1)} %get-tuple-element.13), kind=kOutput, calls=%fused_computation.5 | convolution fusion | flops 1078067200 | bytes 8912896 | tf_op jit(solution)/shard_map/dot_general | solution.py:42
  99.1 0.0 reduce-scatter.10.cloned.1.call-start
  99.1 5.4 %fusion.3 = bf16[8192,256]{0,1:T(8,128)(2,1)} fusion(bf16[256,256]{0,1:T(8,128)(2,1)S(1)} %get-tuple-element.12, bf16[256,8192]{1,0:T(8,128)(2,1)} %param.6), kind=kOutput, calls=%fused_computation.6 | convolution fusion | flops 1077936128 | bytes 8519680 | tf_op jit(solution)/shard_map/dot_general | solution.py:40
  104.6 5.5 %convolution_convert_fusion = bf16[256,8192]{1,0:T(8,128)(2,1)} fusion(bf16[256,256]{0,1:T(8,128)(2,1)S(1)} %get-tuple-element.12, bf16[8192,256]{1,0:T(8,128)(2,1)} %param.9), kind=kOutput, calls=%fused_computation.2 | convolution fusion | flops 1075838976 | bytes 8519680 | tf_op jit(solution)/shard_map/dot_general | solution.py:24
  110.2 18.7 %psum.7 = f32[256]{0:T(256)S(1)} all-reduce(f32[256]{0:T(256)S(1)} %get-tuple-element.10), channel_id=1, replica_groups=mesh['dp'=4,'term'=8] {'term'}, use_global_device_ids=true, to_apply=%region_5.0 | all-reduce | flops 256 | bytes 2048 | tf_op jit(solution)/shard_map/psum | solution.py:22
  128.9 1.4 convert_element_type.61
  130.3 45.6 %reduce-scatter.8.cloned.1.call-done = bf16[256,32]{0,1:T(8,128)(2,1)} async-done(((bf16[256,256]{0,1:T(8,128)(2,1)}), bf16[256,32]{0,1:T(8,128)(2,1)}) %reduce-scatter.8.cloned.1.call-update) | async-done | bytes 16400 | tf_op jit(solution)/shard_map/reduce_scatter | solution.py:30
  175.9 1.3 subtract_multiply_fusion
  177.2 44.8 %reduce-scatter.12.cloned.1.call-done = bf16[2048,256]{0,1:T(8,128)(2,1)} async-done(((bf16[8192,256]{0,1:T(8,128)(2,1)}), bf16[2048,256]{0,1:T(8,128)(2,1)}) %reduce-scatter.12.cloned.1.call-update) | async-done | bytes 1048592 | tf_op jit(solution)/shard_map/reduce_scatter | solution.py:51
  222.0 2.6 copy.13
  224.6 44.4 %reduce-scatter.10.cloned.1.call-done = bf16[2048,256]{0,1:T(8,128)(2,1)} async-done(((bf16[8192,256]{0,1:T(8,128)(2,1)}), bf16[2048,256]{0,1:T(8,128)(2,1)}) %reduce-scatter.10.cloned.1.call-update) | async-done | bytes 1048592 | tf_op jit(solution)/shard_map/reduce_scatter | solution.py:48
  268.9 2.6 copy.12
  271.5 90.3 %reduce-scatter.6.cloned.1.call-done = bf16[256,1024]{1,0:T(8,128)(2,1)} async-done(((bf16[256,8192]{1,0:T(8,128)(2,1)}), bf16[256,1024]{1,0:T(8,128)(2,1)}) %reduce-scatter.6.cloned.1.call-update) | async-done | bytes 524304 | tf_op jit(solution)/shard_map/reduce_scatter | solution.py:27
  (13 shorter events, 0.3 us)
Async XLA Ops:
  7.2 84.4 %copy-start = (bf16[256,256]{1,0:T(8,128)(2,1)S(1)}, bf16[256,256]{1,0:T(8,128)(2,1)}, u32[]{:S(2)}) copy-start(bf16[256,256]{1,0:T(8,128)(2,1)} %param.11) | copy-start | bytes 393220
  7.2 79.1 %all-gather.2.cloned.1.call-start = ((), (), s32[]{:S(2)}) async-start(), calls=%async_computation.5 | async-start | bytes 4718592 | tf_op jit(solution)/shard_map/all_gather | solution.py:18
  7.9 121.0 %reduce-scatter.14.cloned.1.call-start = ((), (), s32[]{:S(2)}) async-start(), calls=%async_computation.10 | async-start | bytes 163840 | tf_op jit(solution)/shard_map/reduce_scatter | solution.py:54
  92.7 83.2 %reduce-scatter.8.cloned.1.call-start = ((), (), s32[]{:S(2)}) async-start(), calls=%async_computation.7 | async-start | bytes 147456 | tf_op jit(solution)/shard_map/reduce_scatter | solution.py:30
  93.6 128.4 %reduce-scatter.12.cloned.1.call-start = ((), (), s32[]{:S(2)}) async-start(), calls=%async_computation.9 | async-start | bytes 5242880 | tf_op jit(solution)/shard_map/reduce_scatter | solution.py:51
  99.1 169.8 %reduce-scatter.10.cloned.1.call-start = ((), (), s32[]{:S(2)}) async-start(), calls=%async_computation.8 | async-start | bytes 5242880 | tf_op jit(solution)/shard_map/reduce_scatter | solution.py:48
  104.6 257.2 %reduce-scatter.6.cloned.1.call-start = ((), (), s32[]{:S(2)}) async-start(), calls=%async_computation.6 | async-start | bytes 4718592 | tf_op jit(solution)/shard_map/reduce_scatter | solution.py:27
Sparse Core Ops, SparseCore 0:
  10.2 76.0 all-gather.1
  92.8 17.8 reduce-scatter.13
  114.9 60.8 reduce-scatter.7
  178.4 43.5 reduce-scatter.11
  224.4 44.4 reduce-scatter.9
  273.4 88.2 reduce-scatter.5
where the time goes:
time: 369 us
  waiting for transfers between devices  297 us (80%)
  matrix products  28.7 us (8%)
  blocking collectives  18.7 us (5%)
  between operations  14.2 us (4%)
  local copies, waits for them, and re-layouts  6.21 us (2%)
  other arithmetic  3.91 us (1%)
    reduce_scatter x1, waiting for transfers between devices, per_device(): lax.psum_scatter(part_x.astype(jnp.bfloat16), 'term', scatter_dimension=1...  90.3 us
    all_gather x1, waiting for transfers between devices, per_device(): full_cotan = lax.all_gather(cotangent, 'term', axis=1, tiled=True)  70.9 us
    reduce_scatter x1, waiting for transfers between devices, per_device(): lax.psum_scatter(part_g.astype(jnp.bfloat16), 'term', scatter_dimension=1...  45.6 us
    reduce_scatter x1, waiting for transfers between devices, per_device(): lax.psum_scatter(part_out.astype(jnp.bfloat16), 'dp', scatter_dimension=0...  44.8 us
    reduce_scatter x1, waiting for transfers between devices, per_device(): lax.psum_scatter(part_in.astype(jnp.bfloat16), 'dp', scatter_dimension=0,...  44.4 us
    psum x1, blocking collectives, per_device(): lax.psum(jnp.sum(grad_hid * proj_in * proj_exp, axis=1, keepdims=True), '...  18.7 us
  transfers between devices with their start and end apart: 6, of which 5 were waited for; matrix products, arithmetic and copies ran while one was open for 9% of the time, Pallas kernels for 0%

commit v1 on v0

--- a/solution.py
+++ b/solution.py
@@ -1,12 +1,343 @@
+import functools
 import math
 
 import jax
 import jax.numpy as jnp
 from jax import lax
+from jax.experimental import pallas as pl
+from jax.experimental.pallas import tpu as pltpu
 from jax.sharding import PartitionSpec as P
 
-
-def per_device(inputs, cotangent, logits, in_factor, out_factor, expert_factor):
+FL = jnp.float32
+BF = jnp.bfloat16
+LAST = (((1,), (1,)), ((), ()))
+FIRST = (((0,), (0,)), ((), ()))
+SUBS = 2
+
+
+def fused_kernel(
+    n, m, scale,
+    x_hbm, cot_ref, log_ref, fin_hbm, fout_hbm, fexp_ref,
+    gx_ref, gl_ref, gin_ref, gout_ref, gexp_ref,
+    x, fin, fout, cot, pin, pexp, ghid, hid, gpin, gpexp, gt, gbf,
+    rs_send, rs_recv, c_send, c_recv, x_send, x_recv,
+    g_send, g_recv, r_send, r_recv, e_send, e_recv,
+    load_sem, ag_s, ag_r, rs_s, rs_r, c_s, c_r, xs_s, xs_r, g_s, g_r, r_s, r_r, e_s, e_r,
+):
+    t = lax.axis_index("term")
+    a = lax.axis_index("dp")
+    tok = cot_ref.shape[0]
+    half = cot_ref.shape[1] // 2
+    rows = tok // SUBS
+    loads = [
+        pltpu.make_async_copy(src, dst, load_sem.at[i])
+        for i, (src, dst) in enumerate(((x_hbm, x), (fin_hbm, fin), (fout_hbm, fout)))
+    ]
+    for c in loads:
+        c.start()
+    barrier = pltpu.get_barrier_semaphore()
+    for d in range(1, n):
+        pl.semaphore_signal(barrier, inc=1, device_id={"term": lax.rem(t + d, n)}, device_id_type=pl.DeviceIdType.MESH)
+    for d in range(1, m):
+        pl.semaphore_signal(barrier, inc=1, device_id={"dp": lax.rem(a + d, m)}, device_id_type=pl.DeviceIdType.MESH)
+    cot[t, 0] = cot_ref[:, :half]
+    cot[t, 1] = cot_ref[:, half:]
+
+    hz = n // 2
+    pos = t // 2 + lax.rem(t, 2) * (n - 1 - 2 * (t // 2))
+
+    def term_at(p):
+        p = lax.rem(p + 2 * n, n)
+        u = p // hz
+        return (1 - u) * 2 * p + u * (2 * (n - 1 - p) + 1)
+
+    ahead = (term_at(pos + 1), term_at(pos - 1))
+    sign = (1, -1)
+    streams = [(d, s) for d in range(2) for s in range(SUBS)]
+
+    def remote(src, dst, ss, rs, dev):
+        return pltpu.make_async_remote_copy(
+            src_ref=src, dst_ref=dst, send_sem=ss, recv_sem=rs,
+            device_id=dev, device_id_type=pl.DeviceIdType.MESH,
+        )
+
+    def ag(d, s, k, owner):
+        ref = cot.at[owner, d, pl.ds(s * rows, rows), :]
+        return remote(ref, ref, ag_s.at[d * SUBS + s, k], ag_r.at[d * SUBS + s, k], {"term": ahead[d]})
+
+    pl.semaphore_wait(barrier, n + m - 2)
+    for d, s in streams:
+        ag(d, s, 0, t).start()
+
+    z = log_ref[...]
+    z = jnp.exp(z - jnp.max(z, axis=1, keepdims=True))
+    gates = z / jnp.sum(z, axis=1, keepdims=True)
+    gt[...] = jnp.transpose(gates)
+    gbf[...] = gates.astype(BF)
+    pexp[...] = jnp.dot(gbf[...], fexp_ref[...], preferred_element_type=FL)
+    loads[0].wait()
+    loads[1].wait()
+    loads[2].wait()
+    pin[...] = jnp.zeros_like(pin)
+    wide = 2 * half
+
+    @pl.loop(0, n)
+    def _(i):
+        at = pl.ds(pl.multiple_of(i * wide, wide), wide)
+        pin[...] += jnp.dot(x[:, at], fin[at, :], preferred_element_type=FL)
+
+    hid[...] = (pin[...] * pexp[...]).astype(BF)
+    ghid[...] = jnp.zeros_like(ghid)
+
+    def add_hid(d, owner):
+        at = pl.ds(pl.multiple_of(owner * wide + d * half, half), half)
+        ghid[...] += jnp.dot(cot[owner, d], fout[at, :], preferred_element_type=FL)
+
+    add_hid(0, t)
+    add_hid(1, t)
+
+    @pl.loop(1, n)
+    def _(k):
+        for d, s in streams:
+            owner = term_at(pos - sign[d] * k)
+            ag(d, s, k - 1, owner).wait_recv()
+
+            @pl.when(k < n - 1)
+            def _():
+                ag(d, s, k, owner).start()
+
+        for d in range(2):
+            add_hid(d, term_at(pos - sign[d] * k))
+
+    gh = ghid[...]
+    gpin[...] = (gh * pexp[...]).astype(BF)
+    ghp = gh * pin[...]
+    gpexp[...] = ghp.astype(BF)
+
+    def part_x(d, s, owner):
+        at = pl.ds(pl.multiple_of(owner * wide + d * half, half), half)
+        return lax.dot_general(gpin[s * rows:(s + 1) * rows, :], fin[at, :], LAST, preferred_element_type=FL)
+
+    def rs(d, s, k):
+        i = d * SUBS + s
+        return remote(rs_send.at[i, k], rs_recv.at[i, k], rs_s.at[i, k], rs_r.at[i, k], {"term": ahead[d]})
+
+    for d, s in streams:
+        rs_send[d * SUBS + s, 0] = part_x(d, s, term_at(pos - sign[d])).astype(BF)
+        rs(d, s, 0).start()
+
+    def rs_step(k):
+        for d, s in streams:
+            i = d * SUBS + s
+            own = part_x(d, s, term_at(pos - sign[d] * (k + 1)))
+            rs(d, s, k - 1).wait_recv()
+            rs_send[i, k] = (own + rs_recv[i, k - 1].astype(FL)).astype(BF)
+            rs(d, s, k).start()
+
+    core = lax.rem(a, 2)
+    xx = a // 2
+    mate = {"dp": 2 * xx + 1 - core}
+    across = {"dp": lax.rem(a + 2, m)}
+    per = gin_ref.shape[0]
+    cuts = per // half
+
+    def part_f(w, owner, j):
+        if w == 0:
+            at = owner * (n // m) + j // 2
+            lhs, rhs = cot[at, lax.rem(j, 2)], hid[...]
+        else:
+            lhs, rhs = x[:, pl.ds(pl.multiple_of(owner * per + j * half, half), half)], gpin[...]
+        return lax.dot_general(lhs, rhs, FIRST, preferred_element_type=FL) * scale
+
+    def to_mate(w, q, j):
+        i = w * cuts + j
+        return remote(c_send.at[q, i], c_recv.at[q, i], c_s.at[q, i], c_r.at[q, i], mate)
+
+    def to_x(w, j):
+        i = w * cuts + j
+        return remote(x_send.at[i], x_recv.at[i], xs_s.at[i], xs_r.at[i], across)
+
+    def give(w, q, chip):
+        @pl.loop(0, cuts)
+        def _(j):
+            c_send[q, w * cuts + j] = part_f(w, 2 * chip + 1 - core, j).astype(BF)
+            to_mate(w, q, j).start()
+
+    def pass_on(w):
+        @pl.loop(0, cuts)
+        def _(j):
+            own = part_f(w, 2 * (1 - xx) + core, j)
+            to_mate(w, 0, j).wait_recv()
+            x_send[w * cuts + j] = (own + c_recv[0, w * cuts + j].astype(FL)).astype(BF)
+            to_x(w, j).start()
+
+    outs = (gout_ref, gin_ref)
+
+    def keep(w):
+        @pl.loop(0, cuts)
+        def _(j):
+            own = part_f(w, a, j)
+            to_mate(w, 1, j).wait_recv()
+            at = pl.ds(pl.multiple_of(j * half, half), half)
+            outs[w][at, :] = own + c_recv[1, w * cuts + j].astype(FL)
+
+    def finish(w):
+        @pl.loop(0, cuts)
+        def _(j):
+            to_x(w, j).wait_recv()
+            at = pl.ds(pl.multiple_of(j * half, half), half)
+            outs[w][at, :] += x_recv[w * cuts + j].astype(FL)
+
+    give(0, 0, 1 - xx)
+    pass_on(0)
+    rs_step(1)
+    give(1, 0, 1 - xx)
+    pass_on(1)
+    rs_step(2)
+
+    share = gt.shape[0] // n
+    row = jnp.sum(ghp * pexp[...], axis=1, keepdims=True)
+    r_send[...] = jnp.transpose(jnp.broadcast_to(row, (tok, 128)))[:8]
+    g_send[...] = lax.dot_general(fexp_ref[...], gpexp[...], LAST, preferred_element_type=FL).astype(BF)
+    e_send[...] = (lax.dot_general(gbf[...], gpexp[...], FIRST, preferred_element_type=FL) * scale).astype(BF)
+    eper = gexp_ref.shape[0]
+
+    def g_copy(d):
+        to = lax.rem(t + d, n)
+        src = g_send.at[pl.ds(pl.multiple_of(to * share, share), share), :]
+        return remote(src, g_recv.at[d - 1], g_s.at[d - 1], g_r.at[d - 1], {"term": to})
+
+    def r_copy(d):
+        return remote(r_send, r_recv.at[d - 1], r_s.at[d - 1], r_r.at[d - 1], {"term": lax.rem(t + d, n)})
+
+    def e_copy(d):
+        to = lax.rem(a + d, m)
+        src = e_send.at[pl.ds(pl.multiple_of(to * eper, eper), eper), :]
+        return remote(src, e_recv.at[d - 1], e_s.at[d - 1], e_r.at[d - 1], {"dp": to})
+
+    for d in range(1, n):
+        g_copy(d).start()
+        r_copy(d).start()
+    for d in range(1, m):
+        e_copy(d).start()
+
+    rs_step(3)
+    give(0, 1, xx)
+    give(1, 1, xx)
+    rs_step(4)
+    keep(0)
+    keep(1)
+    rs_step(5)
+    mine = pl.ds(pl.multiple_of(t * share, share), share)
+    gsum = g_send[mine, :].astype(FL)
+    rsum = r_send[...]
+    for d in range(1, n):
+        g_copy(d).wait_recv()
+        r_copy(d).wait_recv()
+        gsum += g_recv[d - 1].astype(FL)
+        rsum += r_recv[d - 1]
+    gl_ref[...] = gt[mine, :] * (gsum - rsum[:1])
+    esum = e_send[pl.ds(pl.multiple_of(a * eper, eper), eper), :].astype(FL)
+    for d in range(1, m):
+        e_copy(d).wait_recv()
+        esum += e_recv[d - 1].astype(FL)
+    gexp_ref[...] = esum
+    for k in range(6, n - 1):
+        rs_step(k)
+    finish(0)
+    finish(1)
+    for d, s in streams:
+        i = d * SUBS + s
+        own = part_x(d, s, t)
+        rs(d, s, n - 2).wait_recv()
+        gx_ref[s * rows:(s + 1) * rows, d * half:(d + 1) * half] = (own + rs_recv[i, n - 2].astype(FL)).astype(BF)
+
+    @pl.loop(0, n - 1)
+    def _(k):
+        for d, s in streams:
+            ag(d, s, k, term_at(pos - sign[d] * k)).wait_send()
+            rs(d, s, k).wait_send()
+
+    for w in range(2):
+        @pl.loop(0, cuts)
+        def _(j):
+            to_mate(w, 0, j).wait_send()
+            to_mate(w, 1, j).wait_send()
+            to_x(w, j).wait_send()
+
+    for d in range(1, n):
+        g_copy(d).wait_send()
+        r_copy(d).wait_send()
+    for d in range(1, m):
+        e_copy(d).wait_send()
+
+
+def fused(inputs, cotangent, logits, in_factor, out_factor, expert_factor):
+    n, m = lax.axis_size("term"), lax.axis_size("dp")
+    tok, wide = cotangent.shape
+    width, rank = in_factor.shape
+    experts = logits.shape[1]
+    half, rows, per = wide // 2, tok // SUBS, width // m
+    cuts = per // half
+    ns = 2 * SUBS
+    scale = 1.0 / math.sqrt(tok * m)
+    shape = jax.ShapeDtypeStruct
+    vm = pl.BlockSpec(memory_space=pltpu.VMEM)
+    hbm = pl.BlockSpec(memory_space=pl.ANY)
+    dma = pltpu.SemaphoreType.DMA
+    out = pl.pallas_call(
+        functools.partial(fused_kernel, n, m, scale),
+        out_shape=(
+            shape((tok, wide), BF),
+            shape((experts // n, tok), FL),
+            shape((per, rank), FL),
+            shape((per, rank), FL),
+            shape((experts // m, rank), FL),
+        ),
+        in_specs=[hbm, vm, vm, hbm, hbm, vm],
+        out_specs=(vm,) * 5,
+        scratch_shapes=[
+            pltpu.VMEM((tok, width), BF),
+            pltpu.VMEM((width, rank), BF),
+            pltpu.VMEM((width, rank), BF),
+            pltpu.VMEM((n, 2, tok, half), BF),
+            pltpu.VMEM((tok, rank), FL),
+            pltpu.VMEM((tok, rank), FL),
+            pltpu.VMEM((tok, rank), FL),
+            pltpu.VMEM((tok, rank), BF),
+            pltpu.VMEM((tok, rank), BF),
+            pltpu.VMEM((tok, rank), BF),
+            pltpu.VMEM((experts, tok), FL),
+            pltpu.VMEM((tok, experts), BF),
+            pltpu.VMEM((ns, n - 1, rows, half), BF),
+            pltpu.VMEM((ns, n - 1, rows, half), BF),
+            pltpu.VMEM((2, 2 * cuts, half, rank), BF),
+            pltpu.VMEM((2, 2 * cuts, half, rank), BF),
+            pltpu.VMEM((2 * cuts, half, rank), BF),
+            pltpu.VMEM((2 * cuts, half, rank), BF),
+            pltpu.VMEM((experts, tok), BF),
+            pltpu.VMEM((n - 1, experts // n, tok), BF),
+            pltpu.VMEM((8, tok), FL),
+            pltpu.VMEM((n - 1, 8, tok), FL),
+            pltpu.VMEM((experts, rank), BF),
+            pltpu.VMEM((m - 1, experts // m, rank), BF),
+            dma((3,)),
+            dma((ns, n - 1)), dma((ns, n - 1)), dma((ns, n - 1)), dma((ns, n - 1)),
+            dma((2, 2 * cuts)), dma((2, 2 * cuts)), dma((2 * cuts,)), dma((2 * cuts,)),
+            dma((n - 1,)), dma((n - 1,)), dma((n - 1,)), dma((n - 1,)),
+            dma((m - 1,)), dma((m - 1,)),
+        ],
+        compiler_params=pltpu.CompilerParams(
+            collective_id=0, has_side_effects=True, vmem_limit_bytes=60 * 2**20
+        ),
+        cost_estimate=pl.CostEstimate(
+            flops=10 * tok * width * rank, bytes_accessed=8 * width * rank, transcendentals=tok * experts
+        ),
+    )(inputs, cotangent, logits, in_factor, out_factor, expert_factor)
+    return out[0], out[1].T, out[2], out[3], out[4]
+
+
+def by_collectives(inputs, cotangent, logits, in_factor, out_factor, expert_factor):
     fl = jnp.float32
     n_term = lax.axis_size("term")
     n_data = lax.axis_size("dp")
@@ -60,7 +391,7 @@
 
 def solution(mesh):
     return jax.shard_map(
-        per_device,
+        fused if (mesh.shape["term"], mesh.shape["dp"]) == (8, 4) else by_collectives,
         mesh=mesh,
         in_specs=(
             P("dp", None),

time: 369 us -> 122 us (0.33)
  waiting for transfers between devices: 297 us -> 0 us
  Pallas kernels: 0 us -> 113 us
  matrix products: 28.7 us -> 0 us
  blocking collectives: 18.7 us -> 0 us
  between operations: 14.2 us -> 0.65 us
  other arithmetic: 3.91 us -> 0 us
    reduce_scatter x5 -> x0, waiting for transfers between devices: 225 us -> none  [the longest x1 90.3 us: per_device(): lax.psum_scatter(part_x.astype(jnp.bfloat16), 'term', scatter_dimension=1...]
    pallas_call x0 -> x1, Pallas kernels: none -> 113 us  [fused(): pl.pallas_call(functools.partial(fused_kernel, n, m, scale), out_shape=(s...]
    all_gather x1 -> x0, waiting for transfers between devices: 70.9 us -> none  [per_device(): full_cotan = lax.all_gather(cotangent, 'term', axis=1, tiled=True)]
    dot_general x8 -> x0, matrix products: 28.7 us -> none  [the longest x1 5.49 us: per_device(): lax.dot_general(grad_pin, in_factor, contract_last, preferred_element_typ...]
    psum x1 -> x0, blocking collectives: 18.7 us -> none  [per_device(): lax.psum(jnp.sum(grad_hid * proj_in * proj_exp, axis=1, keepdims=True), '...]
    unnamed x5 -> x9, local copies, waits for them, and re-layouts: 6.21 us -> 8.39 us
  transfers between devices with their start and end apart: 6 -> 0, of which waited for: 5 -> 0; matrix products, arithmetic and copies ran while one was open for 9% -> 0% of each run, Pallas kernels for 0% -> 0%
where the time goes in v1:
time: 122 us
  Pallas kernels  113 us (93%)
  local copies, waits for them, and re-layouts  8.39 us (7%)
    pallas_call x1, Pallas kernels, fused(): pl.pallas_call(functools.partial(fused_kernel, n, m, scale), out_shape=(s...  113 us
    unnamed x9, local copies, waits for them, and re-layouts  8.39 us

profile of v1, /device:TPU:0, one launch (start us, length us, event | category | flops | bytes accessed | tf_op | source)
XLA Modules:
  0.0 121.8 jit_solution(14526342767294780320)
XLA Ops:
  0.6 112.7 %shard_map.101 = (bf16[256,1024]{1,0:T(8,128)(2,1)}, f32[32,256]{1,0:T(8,128)}, f32[2048,256]{1,0:T(8,128)}, f32[2048,256]{1,0:T(8,128)}, f32[64,256]{1,0:T(8,128)}) custom-call(bf16[256,8192]{1,0:T(8,128)(2,1)} %x_hbm.1, bf16[256,1024]{1,0:T(8,128)(2,1)} %cot_ref.1, f32[256,256]{1,0:T(8,128)} %log_ref.1, bf16[8192,256]{1,0:T(8,128)(2,1)} %fin_hbm.1, ...), custom_call_target="tpu_custom_call" | custom-call | flops 5368709120 | bytes 16777216 | tf_op jit(solution)/shard_map/pallas_call | solution.py:288
  113.4 1.9 %copy.16 = bf16[256,1024]{1,0:T(8,128)(2,1)} copy(bf16[256,1024]{1,0:T(8,128)(2,1)} %get-tuple-element.20) | data formatting | bytes 1048576
  115.2 1.4 %copy.17 = f32[256,32]{0,1:T(8,128)} copy(f32[256,32]{0,1:T(8,128)} %bitcast.1) | data formatting | bytes 65536
  116.6 0.0 copy-start
  116.6 3.2 %copy.18 = f32[2048,256]{1,0:T(8,128)} copy(f32[2048,256]{1,0:T(8,128)} %get-tuple-element.22) | data formatting | bytes 4194304
  119.8 0.0 copy-done
  119.8 0.0 copy-start.1
  119.8 1.3 %copy.19 = f32[2048,256]{1,0:T(8,128)} copy(f32[2048,256]{1,0:T(8,128)S(1)} %copy-done) | data formatting | bytes 4194304
  121.1 0.0 copy-done.1
  121.1 0.6 copy.20
Async XLA Ops:
  116.6 3.2 %copy-start = (f32[2048,256]{1,0:T(8,128)S(1)}, f32[2048,256]{1,0:T(8,128)}, u32[]{:S(2)}) copy-start(f32[2048,256]{1,0:T(8,128)} %get-tuple-element.23) | copy-start | bytes 6291460
  119.8 1.3 %copy-start.1 = (f32[64,256]{1,0:T(8,128)S(1)}, f32[64,256]{1,0:T(8,128)}, u32[]{:S(2)}) copy-start(f32[64,256]{1,0:T(8,128)} %get-tuple-element.24) | copy-start | bytes 196612

commit v2 on v1

--- a/solution.py
+++ b/solution.py
@@ -20,7 +20,7 @@
     x_hbm, cot_ref, log_ref, fin_hbm, fout_hbm, fexp_ref,
     gx_ref, gl_ref, gin_ref, gout_ref, gexp_ref,
     x, fin, fout, cot, pin, pexp, ghid, hid, gpin, gpexp, gt, gbf,
-    rs_send, rs_recv, c_send, c_recv, x_send, x_recv,
+    rs_send, rs_recv, c_send, c_recv, x_send, x_recv, kept,
     g_send, g_recv, r_send, r_recv, e_send, e_recv,
     load_sem, ag_s, ag_r, rs_s, rs_r, c_s, c_r, xs_s, xs_r, g_s, g_r, r_s, r_r, e_s, e_r,
 ):
@@ -96,6 +96,92 @@
     add_hid(0, t)
     add_hid(1, t)
 
+    core = lax.rem(a, 2)
+    xx = a // 2
+    mate = {"dp": 2 * xx + 1 - core}
+    across = {"dp": lax.rem(a + 2, m)}
+    per = gin_ref.shape[0]
+    cuts = per // half
+
+    def part_f(w, owner, j):
+        if w == 0:
+            at = owner * (n // m) + j // 2
+            lhs, rhs = cot[at, lax.rem(j, 2)], hid[...]
+        else:
+            lhs, rhs = x[:, pl.ds(pl.multiple_of(owner * per + j * half, half), half)], gpin[...]
+        return lax.dot_general(lhs, rhs, FIRST, preferred_element_type=FL) * scale
+
+    def to_mate(w, q, j):
+        i = w * cuts + j
+        return remote(c_send.at[q, i], c_recv.at[q, i], c_s.at[q, i], c_r.at[q, i], mate)
+
+    def to_x(w, j):
+        i = w * cuts + j
+        return remote(x_send.at[i], x_recv.at[i], xs_s.at[i], xs_r.at[i], across)
+
+    def give(w, q, j):
+        chip = q * xx + (1 - q) * (1 - xx)
+        c_send[q, w * cuts + j] = part_f(w, 2 * chip + 1 - core, j).astype(BF)
+        to_mate(w, q, j).start()
+
+    def pass_on(w, j):
+        own = part_f(w, 2 * (1 - xx) + core, j)
+        to_mate(w, 0, j).wait_recv()
+        x_send[w * cuts + j] = (own + c_recv[0, w * cuts + j].astype(FL)).astype(BF)
+        to_x(w, j).start()
+
+    outs = (gout_ref, gin_ref)
+
+    def keep(w, j):
+        own = part_f(w, a, j)
+        to_mate(w, 1, j).wait_recv()
+        kept[w * cuts + j] = own + c_recv[1, w * cuts + j].astype(FL)
+
+    def finish(w):
+        @pl.loop(0, cuts)
+        def _(j):
+            to_x(w, j).wait_recv()
+            at = pl.ds(pl.multiple_of(j * half, half), half)
+            outs[w][at, :] = (kept[w * cuts + j] + x_recv[w * cuts + j].astype(FL)).astype(BF)
+
+    def each(f, lo, hi):
+        @pl.loop(lo, hi)
+        def _(j):
+            f(j)
+
+    def place(d, k):
+        at = term_at(pos - sign[d] * k)
+        return at // (n // m), 2 * lax.rem(at, n // m) + d
+
+    def hand(d, k):
+        owner, j = place(d, k)
+
+        @pl.when(lax.rem(owner, 2) != core)
+        def _():
+            @pl.when(owner // 2 == xx)
+            def _():
+                give(0, 1, j)
+
+            @pl.when(owner // 2 != xx)
+            def _():
+                give(0, 0, j)
+
+    def settle(d, k):
+        owner, j = place(d, k)
+
+        @pl.when(lax.rem(owner, 2) == core)
+        def _():
+            @pl.when(owner // 2 == xx)
+            def _():
+                keep(0, j)
+
+            @pl.when(owner // 2 != xx)
+            def _():
+                pass_on(0, j)
+
+    hand(0, 0)
+    hand(1, 0)
+
     @pl.loop(1, n)
     def _(k):
         for d, s in streams:
@@ -108,6 +194,10 @@
 
         for d in range(2):
             add_hid(d, term_at(pos - sign[d] * k))
+        for d in range(2):
+            hand(d, k)
+        for d in range(2):
+            settle(d, k - 1)
 
     gh = ghid[...]
     gpin[...] = (gh * pexp[...]).astype(BF)
@@ -134,65 +224,12 @@
             rs_send[i, k] = (own + rs_recv[i, k - 1].astype(FL)).astype(BF)
             rs(d, s, k).start()
 
-    core = lax.rem(a, 2)
-    xx = a // 2
-    mate = {"dp": 2 * xx + 1 - core}
-    across = {"dp": lax.rem(a + 2, m)}
-    per = gin_ref.shape[0]
-    cuts = per // half
-
-    def part_f(w, owner, j):
-        if w == 0:
-            at = owner * (n // m) + j // 2
-            lhs, rhs = cot[at, lax.rem(j, 2)], hid[...]
-        else:
-            lhs, rhs = x[:, pl.ds(pl.multiple_of(owner * per + j * half, half), half)], gpin[...]
-        return lax.dot_general(lhs, rhs, FIRST, preferred_element_type=FL) * scale
-
-    def to_mate(w, q, j):
-        i = w * cuts + j
-        return remote(c_send.at[q, i], c_recv.at[q, i], c_s.at[q, i], c_r.at[q, i], mate)
-
-    def to_x(w, j):
-        i = w * cuts + j
-        return remote(x_send.at[i], x_recv.at[i], xs_s.at[i], xs_r.at[i], across)
-
-    def give(w, q, chip):
-        @pl.loop(0, cuts)
-        def _(j):
-            c_send[q, w * cuts + j] = part_f(w, 2 * chip + 1 - core, j).astype(BF)
-            to_mate(w, q, j).start()
-
-    def pass_on(w):
-        @pl.loop(0, cuts)
-        def _(j):
-            own = part_f(w, 2 * (1 - xx) + core, j)
-            to_mate(w, 0, j).wait_recv()
-            x_send[w * cuts + j] = (own + c_recv[0, w * cuts + j].astype(FL)).astype(BF)
-            to_x(w, j).start()
-
-    outs = (gout_ref, gin_ref)
-
-    def keep(w):
-        @pl.loop(0, cuts)
-        def _(j):
-            own = part_f(w, a, j)
-            to_mate(w, 1, j).wait_recv()
-            at = pl.ds(pl.multiple_of(j * half, half), half)
-            outs[w][at, :] = own + c_recv[1, w * cuts + j].astype(FL)
-
-    def finish(w):
-        @pl.loop(0, cuts)
-        def _(j):
-            to_x(w, j).wait_recv()
-            at = pl.ds(pl.multiple_of(j * half, half), half)
-            outs[w][at, :] += x_recv[w * cuts + j].astype(FL)
-
-    give(0, 0, 1 - xx)
-    pass_on(0)
+    each(lambda j: give(1, 0, j), 0, cuts)
+    each(lambda j: pass_on(1, j), 0, cuts // 2)
     rs_step(1)
-    give(1, 0, 1 - xx)
-    pass_on(1)
+    each(lambda j: pass_on(1, j), cuts // 2, cuts)
+    settle(0, n - 1)
+    settle(1, n - 1)
     rs_step(2)
 
     share = gt.shape[0] // n
@@ -222,12 +259,11 @@
         e_copy(d).start()
 
     rs_step(3)
-    give(0, 1, xx)
-    give(1, 1, xx)
+    each(lambda j: give(1, 1, j), 0, cuts)
     rs_step(4)
-    keep(0)
-    keep(1)
+    finish(0)
     rs_step(5)
+    each(lambda j: keep(1, j), 0, cuts)
     mine = pl.ds(pl.multiple_of(t * share, share), share)
     gsum = g_send[mine, :].astype(FL)
     rsum = r_send[...]
@@ -244,7 +280,6 @@
     gexp_ref[...] = esum
     for k in range(6, n - 1):
         rs_step(k)
-    finish(0)
     finish(1)
     for d, s in streams:
         i = d * SUBS + s
@@ -290,8 +325,8 @@
         out_shape=(
             shape((tok, wide), BF),
             shape((experts // n, tok), FL),
-            shape((per, rank), FL),
-            shape((per, rank), FL),
+            shape((per, rank), BF),
+            shape((per, rank), BF),
             shape((experts // m, rank), FL),
         ),
         in_specs=[hbm, vm, vm, hbm, hbm, vm],
@@ -315,6 +350,7 @@
             pltpu.VMEM((2, 2 * cuts, half, rank), BF),
             pltpu.VMEM((2 * cuts, half, rank), BF),
             pltpu.VMEM((2 * cuts, half, rank), BF),
+            pltpu.VMEM((2 * cuts, half, rank), FL),
             pltpu.VMEM((experts, tok), BF),
             pltpu.VMEM((n - 1, experts // n, tok), BF),
             pltpu.VMEM((8, tok), FL),
@@ -334,7 +370,7 @@
             flops=10 * tok * width * rank, bytes_accessed=8 * width * rank, transcendentals=tok * experts
         ),
     )(inputs, cotangent, logits, in_factor, out_factor, expert_factor)
-    return out[0], out[1].T, out[2], out[3], out[4]
+    return out[0], out[1].T, out[2].astype(FL), out[3].astype(FL), out[4]
 
 
 def by_collectives(inputs, cotangent, logits, in_factor, out_factor, expert_factor):

time: 122 us -> 110 us (0.902)
  Pallas kernels: 113 us -> 102 us
  local copies, waits for them, and re-layouts: 8.39 us -> 2.05 us
  other arithmetic: 0 us -> 5.46 us
    pallas_call x1, Pallas kernels: 113 us -> 102 us  [fused(): pl.pallas_call(functools.partial(fused_kernel, n, m, scale), out_shape=(s...]
    unnamed x9, local copies, waits for them, and re-layouts: 8.39 us -> 2.05 us
    convert_element_type x0 -> x2, other arithmetic: none -> 5.46 us  [fused(): return (out[0], out[1].T, out[2].astype(FL), out[3].astype(FL), out[4])]
where the time goes in v2:
time: 110 us
  Pallas kernels  102 us (93%)
  other arithmetic  5.46 us (5%)
  local copies, waits for them, and re-layouts  2.05 us (2%)
    pallas_call x1, Pallas kernels, fused(): pl.pallas_call(functools.partial(fused_kernel, n, m, scale), out_shape=(s...  102 us
    convert_element_type x2, other arithmetic, fused(): return (out[0], out[1].T, out[2].astype(FL), out[3].astype(FL), out[4])  5.46 us

profile of v2, /device:TPU:0, one launch (start us, length us, event | category | flops | bytes accessed | tf_op | source)
XLA Modules:
  0.0 109.7 jit_solution(4430717201482204196)
XLA Ops:
  0.6 101.6 %shard_map.101 = (bf16[256,1024]{1,0:T(8,128)(2,1)}, f32[32,256]{1,0:T(8,128)}, bf16[2048,256]{1,0:T(8,128)(2,1)}, bf16[2048,256]{1,0:T(8,128)(2,1)}, f32[64,256]{1,0:T(8,128)}) custom-call(bf16[256,8192]{1,0:T(8,128)(2,1)} %x_hbm.1, bf16[256,1024]{1,0:T(8,128)(2,1)} %cot_ref.1, f32[256,256]{1,0:T(8,128)} %log_ref.1, bf16[8192,256]{1,0:T(8,128)(2,1)} %fin_hbm.1, ...), custom_call_target="tpu_custom_call" | custom-call | flops 5368709120 | bytes 16777216 | tf_op jit(solution)/shard_map/pallas_call | solution.py:323
  102.2 0.0 copy-start
  102.2 0.0 copy-start.2
  102.2 0.0 copy-start.1
  102.2 2.8 %convert_element_type.6 = f32[2048,256]{1,0:T(8,128)} convert(bf16[2048,256]{1,0:T(8,128)(2,1)} %get-tuple-element.12) | non-fusion elementwise | flops 524288 | bytes 3145728 | tf_op jit(solution)/shard_map/convert_element_type | solution.py:373
  105.0 2.7 %convert_element_type.7 = f32[2048,256]{1,0:T(8,128)} convert(bf16[2048,256]{1,0:T(8,128)(2,1)} %get-tuple-element.13) | non-fusion elementwise | flops 524288 | bytes 3145728 | tf_op jit(solution)/shard_map/convert_element_type | solution.py:373
  107.7 0.0 copy-done
  107.7 0.8 copy.14
  108.5 0.0 copy-done.2
  108.5 0.6 copy.15
  109.1 0.0 copy-done.1
  109.1 0.6 copy.16
Async XLA Ops:
  102.2 5.5 %copy-start = (bf16[256,1024]{1,0:T(8,128)(2,1)S(1)}, bf16[256,1024]{1,0:T(8,128)(2,1)}, u32[]{:S(2)}) copy-start(bf16[256,1024]{1,0:T(8,128)(2,1)} %get-tuple-element.20) | copy-start | bytes 1572868
  102.2 6.3 %copy-start.2 = (f32[32,256]{1,0:T(8,128)S(1)}, f32[32,256]{1,0:T(8,128)}, u32[]{:S(2)}) copy-start(f32[32,256]{1,0:T(8,128)} %get-tuple-element.11) | copy-start | bytes 98308
  102.2 6.9 %copy-start.1 = (f32[64,256]{1,0:T(8,128)S(1)}, f32[64,256]{1,0:T(8,128)}, u32[]{:S(2)}) copy-start(f32[64,256]{1,0:T(8,128)} %get-tuple-element.24) | copy-start | bytes 196612

commit v3 on v2

--- a/solution.py
+++ b/solution.py
@@ -53,7 +53,7 @@
 
     ahead = (term_at(pos + 1), term_at(pos - 1))
     sign = (1, -1)
-    streams = [(d, s) for d in range(2) for s in range(SUBS)]
+    streams = [(d, s) for s in range(SUBS) for d in range(2)]
 
     def remote(src, dst, ss, rs, dev):
         return pltpu.make_async_remote_copy(
@@ -68,6 +68,15 @@
     pl.semaphore_wait(barrier, n + m - 2)
     for d, s in streams:
         ag(d, s, 0, t).start()
+
+    def forward(k):
+        for d, s in streams:
+            owner = term_at(pos - sign[d] * k)
+            ag(d, s, k - 1, owner).wait_recv()
+
+            @pl.when(k < n - 1)
+            def _():
+                ag(d, s, k, owner).start()
 
     z = log_ref[...]
     z = jnp.exp(z - jnp.max(z, axis=1, keepdims=True))
@@ -78,6 +87,7 @@
     loads[0].wait()
     loads[1].wait()
     loads[2].wait()
+    forward(1)
     pin[...] = jnp.zeros_like(pin)
     wide = 2 * half
 
@@ -179,25 +189,26 @@
             def _():
                 pass_on(0, j)
 
-    hand(0, 0)
-    hand(1, 0)
-
-    @pl.loop(1, n)
-    def _(k):
-        for d, s in streams:
-            owner = term_at(pos - sign[d] * k)
-            ag(d, s, k - 1, owner).wait_recv()
-
-            @pl.when(k < n - 1)
-            def _():
-                ag(d, s, k, owner).start()
-
+    def add_both(k):
         for d in range(2):
             add_hid(d, term_at(pos - sign[d] * k))
-        for d in range(2):
-            hand(d, k)
-        for d in range(2):
-            settle(d, k - 1)
+
+    def both(f, k):
+        f(0, k)
+        f(1, k)
+
+    add_both(1)
+    both(hand, 0)
+
+    @pl.loop(2, n - 1)
+    def _(k):
+        forward(k)
+        add_both(k)
+        both(hand, k - 1)
+        both(settle, k - 2)
+
+    forward(n - 1)
+    add_both(n - 1)
 
     gh = ghid[...]
     gpin[...] = (gh * pexp[...]).astype(BF)
@@ -224,12 +235,17 @@
             rs_send[i, k] = (own + rs_recv[i, k - 1].astype(FL)).astype(BF)
             rs(d, s, k).start()
 
-    each(lambda j: give(1, 0, j), 0, cuts)
+    @pl.loop(n - 2, n)
+    def _(k):
+        both(hand, k)
+        both(settle, k - 1)
+
+    each(lambda j: give(1, 0, j), 0, cuts // 2)
+    rs_step(1)
     each(lambda j: pass_on(1, j), 0, cuts // 2)
-    rs_step(1)
+    each(lambda j: give(1, 0, j), cuts // 2, cuts)
+    both(settle, n - 1)
     each(lambda j: pass_on(1, j), cuts // 2, cuts)
-    settle(0, n - 1)
-    settle(1, n - 1)
     rs_step(2)
 
     share = gt.shape[0] // n
@@ -305,6 +321,37 @@
         r_copy(d).wait_send()
     for d in range(1, m):
         e_copy(d).wait_send()
+
+
+def finishing_kernel(gx, gl, gin, gout, gexp, gx_o, gl_o, gin_o, gout_o, gexp_o):
+    gx_o[...] = gx[...]
+    gin_o[...] = gin[...].astype(FL)
+    gout_o[...] = gout[...].astype(FL)
+
+    @pl.when(pl.program_id(0) == 0)
+    def _():
+        gl_o[...] = gl[...]
+        gexp_o[...] = gexp[...]
+
+
+def finishing(gx, gl, gin, gout, gexp):
+    steps = 4
+    cut = lambda v: pl.BlockSpec((v.shape[0] // steps, v.shape[1]), lambda i: (i, 0))
+    full = lambda v: pl.BlockSpec(v.shape, lambda i: (0, 0))
+    specs = [cut(gx), full(gl), cut(gin), cut(gout), full(gexp)]
+    shape = jax.ShapeDtypeStruct
+    out = pl.pallas_call(
+        finishing_kernel,
+        grid=(steps,),
+        out_shape=(
+            shape(gx.shape, BF), shape(gl.shape, FL), shape(gin.shape, FL),
+            shape(gout.shape, FL), shape(gexp.shape, FL),
+        ),
+        in_specs=specs,
+        out_specs=specs,
+        compiler_params=pltpu.CompilerParams(vmem_limit_bytes=32 * 2**20),
+    )(gx, gl, gin, gout, gexp)
+    return out[0], out[1].T, out[2], out[3], out[4]
 
 
 def fused(inputs, cotangent, logits, in_factor, out_factor, expert_factor):
@@ -370,7 +417,7 @@
             flops=10 * tok * width * rank, bytes_accessed=8 * width * rank, transcendentals=tok * experts
         ),
     )(inputs, cotangent, logits, in_factor, out_factor, expert_factor)
-    return out[0], out[1].T, out[2].astype(FL), out[3].astype(FL), out[4]
+    return finishing(*out)
 
 
 def by_collectives(inputs, cotangent, logits, in_factor, out_factor, expert_factor):

time: 110 us -> 106 us (0.964)
  other arithmetic: 5.46 us -> 0 us
  local copies, waits for them, and re-layouts: 2.05 us -> 5.08 us
  Pallas kernels: 102 us -> 100 us
    convert_element_type x2 -> x0, other arithmetic: 5.46 us -> none  [fused(): return (out[0], out[1].T, out[2].astype(FL), out[3].astype(FL), out[4])]
    pallas_call x1, Pallas kernels: 102 us -> 97.7 us  [fused(): pl.pallas_call(functools.partial(fused_kernel, n, m, scale), out_shape=(s...]
    unnamed x9 -> x10, local copies, waits for them, and re-layouts: 2.05 us -> 5.08 us
    pallas_call x0 -> x1, Pallas kernels: none -> 2.57 us  [finishing(): pl.pallas_call(finishing_kernel, grid=(steps,), out_shape=(shape(gx.shape...]
where the time goes in v3:
time: 106 us
  Pallas kernels  100 us (94%)
  local copies, waits for them, and re-layouts  5.08 us (5%)
    pallas_call x1, Pallas kernels, fused(): pl.pallas_call(functools.partial(fused_kernel, n, m, scale), out_shape=(s...  97.7 us
    unnamed x10, local copies, waits for them, and re-layouts  5.08 us
    pallas_call x1, Pallas kernels, finishing(): pl.pallas_call(finishing_kernel, grid=(steps,), out_shape=(shape(gx.shape...  2.57 us

profile of v3, /device:TPU:0, one launch (start us, length us, event | category | flops | bytes accessed | tf_op | source)
XLA Modules:
  0.0 106.0 jit_solution(5803378149194237118)
XLA Ops:
  0.6 97.7 %shard_map.101 = (bf16[256,1024]{1,0:T(8,128)(2,1)}, f32[32,256]{1,0:T(8,128)}, bf16[2048,256]{1,0:T(8,128)(2,1)}, bf16[2048,256]{1,0:T(8,128)(2,1)}, f32[64,256]{1,0:T(8,128)}) custom-call(bf16[256,8192]{1,0:T(8,128)(2,1)} %x_hbm.1, bf16[256,1024]{1,0:T(8,128)(2,1)} %cot_ref.1, f32[256,256]{1,0:T(8,128)} %log_ref.1, bf16[8192,256]{1,0:T(8,128)(2,1)} %fin_hbm.1, ...), custom_call_target="tpu_custom_call" | custom-call | flops 5368709120 | bytes 16777216 | tf_op jit(solution)/shard_map/pallas_call | solution.py:370
  98.4 0.0 copy-start
  98.4 1.2 %copy-done = bf16[2048,256]{1,0:T(8,128)(2,1)S(1)} copy-done((bf16[2048,256]{1,0:T(8,128)(2,1)S(1)}, bf16[2048,256]{1,0:T(8,128)(2,1)}, u32[]{:S(2)}) %copy-start) | copy-done | bytes 1048600
  99.6 0.0 copy-start.1
  99.6 1.2 %copy-done.1 = bf16[2048,256]{1,0:T(8,128)(2,1)S(1)} copy-done((bf16[2048,256]{1,0:T(8,128)(2,1)S(1)}, bf16[2048,256]{1,0:T(8,128)(2,1)}, u32[]{:S(2)}) %copy-start.1) | copy-done | bytes 1048600
  100.8 0.0 copy-start.2
  100.8 1.0 copy-done.2
  101.8 0.0 copy-start.3
  101.8 0.8 copy-done.3
  102.7 0.0 copy-start.4
  102.7 0.8 copy-done.4
  103.4 2.6 %shard_map.102 = (bf16[256,1024]{1,0:T(8,128)(2,1)}, f32[32,256]{1,0:T(8,128)}, f32[2048,256]{1,0:T(8,128)}, f32[2048,256]{1,0:T(8,128)}, f32[64,256]{1,0:T(8,128)}) custom-call(bf16[256,1024]{1,0:T(8,128)(2,1)S(1)} %copy-done.2, f32[32,256]{1,0:T(8,128)S(1)} %copy-done.4, bf16[2048,256]{1,0:T(8,128)(2,1)S(1)} %copy-done, bf16[2048,256]{1,0:T(8,128)(2,1)S(1)} %copy-done.1, ...), custom_call_target="tpu_custom_call" | custom-call | tf_op jit(solution)/shard_map/pallas_call | solution.py:343
Async XLA Ops:
  98.4 1.2 %copy-start = (bf16[2048,256]{1,0:T(8,128)(2,1)S(1)}, bf16[2048,256]{1,0:T(8,128)(2,1)}, u32[]{:S(2)}) copy-start(bf16[2048,256]{1,0:T(8,128)(2,1)} %get-tuple-element.17.gin) | copy-start | bytes 3145732
  99.6 1.2 %copy-start.1 = (bf16[2048,256]{1,0:T(8,128)(2,1)S(1)}, bf16[2048,256]{1,0:T(8,128)(2,1)}, u32[]{:S(2)}) copy-start(bf16[2048,256]{1,0:T(8,128)(2,1)} %get-tuple-element.18.gout) | copy-start | bytes 3145732
  100.8 1.0 copy-start.2
  101.8 0.8 copy-start.3
  102.7 0.8 copy-start.4

commit v4 on v3

--- a/solution.py
+++ b/solution.py
@@ -349,7 +349,7 @@
         ),
         in_specs=specs,
         out_specs=specs,
-        compiler_params=pltpu.CompilerParams(vmem_limit_bytes=32 * 2**20),
+        compiler_params=pltpu.CompilerParams(vmem_limit_bytes=60 * 2**20),
     )(gx, gl, gin, gout, gexp)
     return out[0], out[1].T, out[2], out[3], out[4]
 

time: 106 us -> 103 us (0.972)
  local copies, waits for them, and re-layouts: 5.08 us -> 0 us
  Pallas kernels: 100 us -> 102 us
    unnamed x10 -> x0, local copies, waits for them, and re-layouts: 5.08 us -> none
    pallas_call x1, Pallas kernels: 2.57 us -> 4.53 us  [finishing(): pl.pallas_call(finishing_kernel, grid=(steps,), out_shape=(shape(gx.shape...]
where the time goes in v4:
time: 103 us
  Pallas kernels  102 us (99%)
    pallas_call x1, Pallas kernels, fused(): pl.pallas_call(functools.partial(fused_kernel, n, m, scale), out_shape=(s...  97.7 us
    pallas_call x1, Pallas kernels, finishing(): pl.pallas_call(finishing_kernel, grid=(steps,), out_shape=(shape(gx.shape...  4.53 us

profile of v4, /device:TPU:0, one launch (start us, length us, event | category | flops | bytes accessed | tf_op | source)
XLA Modules:
  0.0 102.8 jit_solution(132618545528841057)
XLA Ops:
  0.6 97.7 %shard_map.101 = (bf16[256,1024]{1,0:T(8,128)(2,1)}, f32[32,256]{1,0:T(8,128)}, bf16[2048,256]{1,0:T(8,128)(2,1)}, bf16[2048,256]{1,0:T(8,128)(2,1)}, f32[64,256]{1,0:T(8,128)}) custom-call(bf16[256,8192]{1,0:T(8,128)(2,1)} %x_hbm.1, bf16[256,1024]{1,0:T(8,128)(2,1)} %cot_ref.1, f32[256,256]{1,0:T(8,128)} %log_ref.1, bf16[8192,256]{1,0:T(8,128)(2,1)} %fin_hbm.1, ...), custom_call_target="tpu_custom_call" | custom-call | flops 5368709120 | bytes 16777216 | tf_op jit(solution)/shard_map/pallas_call | solution.py:370
  98.3 4.5 %shard_map.102 = (bf16[256,1024]{1,0:T(8,128)(2,1)}, f32[32,256]{1,0:T(8,128)}, f32[2048,256]{1,0:T(8,128)}, f32[2048,256]{1,0:T(8,128)}, f32[64,256]{1,0:T(8,128)}) custom-call(bf16[256,1024]{1,0:T(8,128)(2,1)} %get-tuple-element.15.gx, f32[32,256]{1,0:T(8,128)} %get-tuple-element.16.gl, bf16[2048,256]{1,0:T(8,128)(2,1)} %get-tuple-element.17.gin, ...), custom_call_target="tpu_custom_call" | custom-call | tf_op jit(solution)/shard_map/pallas_call | solution.py:343
